TPU v7x, 32 devices: a whole 2x2x4 slice. The times are simulated.
32 devices in a mesh: section: 2 (over x), dp: 8 (over z, core), head: 2 (over y).
Axes of the slice: x: 2, y: 2, z: 4, core: 2. Of those that a mesh axis runs over, the one named last changes fastest.
Arguments:
- tokens: bfloat16 [2, 2, 8192, 512], P('section', None, ('dp', 'head')), may hold values from -6 to 6
- self_routes: int32 [2, 2, 8192, 2], P('section', None, 'dp'), may hold values from 0 to 3, all different within a row
- cross_routes: int32 [2, 8192, 2], P(None, 'dp'), may hold values from 0 to 3, all different within a row
- lengths: int32 [2, 2, 8], P(None, None, 'dp'), may hold values from 512 to 1024
- cotangent: bfloat16 [2, 8192, 512], P(None, ('dp', 'head')), may hold values from -6 to 6
- norm_attn: bfloat16 [512], P('dp'), may hold values from 0.5 to 1.5
- norm_ffn: bfloat16 [512], P('dp'), may hold values from 0.5 to 1.5
- norm_final: bfloat16 [512], P('dp'), may hold values from 0.5 to 1.5
- norm_cross: bfloat16 [512], P('dp'), may hold values from 0.5 to 1.5
- router: bfloat16 [512, 4], P('dp'), may hold values from -0.125 to 0.125
- query_weight: bfloat16 [4, 512, 64], P('head', 'dp'), may hold values from -0.25 to 0.25
- key_weight: bfloat16 [512, 64], P('dp'), may hold values from -0.25 to 0.25
- value_weight: bfloat16 [512, 64], P('dp'), may hold values from -0.25 to 0.25
- output_weight: bfloat16 [4, 64, 512], P('head', None, 'dp'), may hold values from -6 to 6
- up_weight: bfloat16 [512, 2048], P('dp', 'head'), may hold values from -0.25 to 0.25
- down_weight: bfloat16 [2048, 512], P('head', 'dp'), may hold values from -0.125 to 0.125
- cross_router: bfloat16 [512, 4], P('dp'), may hold values from -0.125 to 0.125
- cross_query: bfloat16 [4, 512, 64], P('head', 'dp'), may hold values from -0.25 to 0.25
- cross_key: bfloat16 [512, 64], P('dp'), may hold values from -0.25 to 0.25
- cross_value: bfloat16 [512, 64], P('dp'), may hold values from -0.25 to 0.25
- cross_output: bfloat16 [4, 64, 512], P('head', None, 'dp'), may hold values from -6 to 6
Outputs:
- outputs: bfloat16 [2, 2, 8192, 512], P('section', None, ('dp', 'head'))
- input_grads: float32 [2, 2, 8192, 512], P('section', None, ('dp', 'head'))
- grad_norm_attn: float32 [512], P('dp')
- grad_norm_ffn: float32 [512], P('dp')
- grad_norm_final: float32 [512], P('dp')
- grad_norm_cross: float32 [512], P('dp')
- grad_router: float32 [512, 4], P('dp')
- grad_query_weight: float32 [4, 512, 64], P('head', 'dp')
- grad_key_weight: float32 [512, 64], P('dp')
- grad_value_weight: float32 [512, 64], P('dp')
- grad_output_weight: float32 [4, 64, 512], P('head', None, 'dp')
- grad_up_weight: float32 [512, 2048], P('dp', 'head')
- down_weight_gradient: float32 [2048, 512], P('head', 'dp')
- grad_cross_router: float32 [512, 4], P('dp')
- grad_cross_query: float32 [4, 512, 64], P('head', 'dp')
- grad_cross_key: float32 [512, 64], P('dp')
- grad_cross_value: float32 [512, 64], P('dp')
- grad_cross_output: float32 [4, 64, 512], P('head', None, 'dp')
Inputs may be any that keep to these rules, and one draw needn't show every extreme that they name: `self_routes`: each token names two different experts. `cross_routes`: each token names two different experts.
All inputs are finite; a program needn't handle non-finite values.
Results may differ from a plain program's by a relative error of at most 0.024.
Values may be sent and summed in bfloat16 or wider, within the bound.
A program may use at most 256 MiB of HBM per device.

v0:
```python
import math

import jax
import jax.numpy as jnp
from jax import lax
from jax.sharding import PartitionSpec as P

EPSILON = 1e-05
PRECISE = lax.Precision.HIGHEST
NEGATIVE_FAR = -1e30


def shifted(block, axis, distance):
    devices = range(lax.axis_size(axis))
    route = [(i - distance, i) for i in devices if i - distance in devices]
    return lax.ppermute(block, axis, route)


def split_up(value, dim, length):
    before, after = (value.shape[:dim], value.shape[dim + 1 :])
    return jnp.moveaxis(value.reshape(*before, length, -1, *after), dim, 0)


def summed_on_arrival(value, axis, dim):
    blocks = split_up(value, dim, lax.axis_size(axis))
    arrived = lax.all_to_all(blocks, axis, split_axis=0, concat_axis=0, tiled=True)
    return arrived.astype(jnp.float32).sum(axis=0)


def sent_together(arrays, axis, dim, along):
    widths = [math.prod(a.shape[along:]) for a in arrays]
    both = jnp.concatenate(
        [a.reshape(*a.shape[:along], w) for a, w in zip(arrays, widths)], axis=along
    )
    filled = summed_on_arrival(both, axis, dim)
    blocks = jnp.split(filled, [sum(widths[:k]) for k in range(1, len(widths))], axis=along)
    return tuple(
        (b.reshape(*filled.shape[:along], *a.shape[along:]) for a, b in zip(arrays, blocks))
    )


def side_by_side(arrays, axis, dim, along):
    both = jnp.concatenate(arrays, axis=along)
    filled, at, done = (summed_on_arrival(both, axis, dim), 0, [])
    for a in arrays:
        done.append(lax.slice_in_dim(filled, at, at + a.shape[along], axis=along))
        at += a.shape[along]
    return tuple(done)


def layer_norm(rows, gain):
    center = jnp.mean(rows, -1, keepdims=True)
    centred = rows - center
    return centred * lax.rsqrt(jnp.mean(centred * centred, -1, keepdims=True) + EPSILON) * gain


def norm_back(rows, gain, upstream):
    _, pull = jax.vjp(layer_norm, rows, gain)
    return pull(upstream)


def gelu_tanh(hidden):
    return jax.nn.gelu(hidden, approximate=True)


def select_at(array, position):
    return lax.dynamic_index_in_dim(array, position, 0, keepdims=False)


def keep_at(table, position, value, active_flag):
    previous = select_at(table, position)
    return lax.dynamic_update_index_in_dim(
        table, jnp.where(active_flag, value, previous), position, 0
    )


def own_rows(array, head_index, count):
    return lax.dynamic_slice_in_dim(array, head_index * count, count, 0)


def gate_parts(logits, routes):
    onehot = (
        routes[:, :, None] == jnp.arange(logits.shape[1], dtype=jnp.int32)[None, None, :]
    ).astype(jnp.float32)
    chosen = jnp.sum(onehot * logits[:, None, :], -1)
    gate_values = jax.nn.softmax(chosen, -1)
    return (gate_values, onehot, jnp.sum(onehot * gate_values[:, :, None], 1))


def gate_back(gate_values, onehot, grad_grid):
    grad_gates = jnp.sum(onehot * grad_grid[:, None, :], -1)
    grad_chosen = gate_values * (grad_gates - jnp.sum(gate_values * grad_gates, -1, keepdims=True))
    return jnp.sum(onehot * grad_chosen[:, :, None], 1)


def allowed_keys(seq_len, length, causal):
    places = jnp.arange(seq_len, dtype=jnp.int32)
    inside = places[None, :] < length
    earlier = places[None, :] <= places[:, None]
    return inside & (earlier | jnp.logical_not(causal))


def by_sequence(queries, key_rows, value_rows, count):
    experts_local, block_rows, head_size = queries.shape
    seq_len = block_rows // count
    query_seq = jnp.moveaxis(queries.reshape(experts_local, count, seq_len, head_size), 1, 0)
    return (
        query_seq,
        key_rows.reshape(count, seq_len, head_size),
        value_rows.reshape(count, seq_len, head_size),
        seq_len,
    )


def spread_rows(rows):
    return lax.all_gather(rows, "head", axis=0, tiled=True)


def reduce_rows(partial_value):
    return lax.psum_scatter(
        partial_value.astype(jnp.bfloat16), "head", scatter_dimension=0, tiled=True
    ).astype(jnp.float32)


def spread_grads(rows):
    return lax.all_gather(rows, "head", axis=0, tiled=True)


def reduce_grads(partial_value):
    return lax.psum_scatter(
        partial_value.astype(jnp.bfloat16), "head", scatter_dimension=0, tiled=True
    ).astype(jnp.float32)


def attend(queries, key_rows, value_rows, seq_lengths, causal):
    experts_local, block_rows, head_size = queries.shape
    scale = 1.0 / math.sqrt(head_size)
    query_seq, key_seq, value_seq, seq_len = by_sequence(
        queries, key_rows, value_rows, seq_lengths.shape[0]
    )

    def single(pieces):
        query_one, key_one, single_value, length = pieces
        scores = (
            jnp.einsum("eqh,kh->eqk", query_one, key_one, preferred_element_type=jnp.float32)
            * scale
        )
        scores = jnp.where(allowed_keys(seq_len, length, causal)[None], scores, NEGATIVE_FAR)
        highest = jnp.max(scores, -1, keepdims=True)
        log_total = highest + jnp.log(jnp.sum(jnp.exp(scores - highest), -1, keepdims=True))
        chances = jnp.exp(scores - log_total).astype(jnp.bfloat16)
        attended = jnp.einsum(
            "eqk,kh->eqh", chances, single_value, preferred_element_type=jnp.float32
        )
        return (attended, log_total[:, :, 0])

    attended, log_total = lax.map(single, (query_seq, key_seq, value_seq, seq_lengths))
    attended = jnp.moveaxis(attended, 0, 1).reshape(experts_local, block_rows, head_size)
    log_total = jnp.moveaxis(log_total, 0, 1).reshape(experts_local, block_rows)
    return (attended, log_total)


def attend_back(queries, key_rows, value_rows, seq_lengths, causal, log_total, grad_attended):
    experts_local, block_rows, head_size = queries.shape
    scale = 1.0 / math.sqrt(head_size)
    count = seq_lengths.shape[0]
    query_seq, key_seq, value_seq, seq_len = by_sequence(queries, key_rows, value_rows, count)
    sequence_total = jnp.moveaxis(log_total.reshape(experts_local, count, seq_len), 1, 0)
    grad_seq = jnp.moveaxis(grad_attended.reshape(experts_local, count, seq_len, head_size), 1, 0)

    def single(pieces):
        query_one, key_one, single_value, length, total_one, grad_one = pieces
        scores = (
            jnp.einsum("eqh,kh->eqk", query_one, key_one, preferred_element_type=jnp.float32)
            * scale
        )
        scores = jnp.where(allowed_keys(seq_len, length, causal)[None], scores, NEGATIVE_FAR)
        chances = jnp.exp(scores - total_one[:, :, None])
        grad_chances = jnp.einsum(
            "eqh,kh->eqk", grad_one, single_value, preferred_element_type=jnp.float32
        )
        grad_scores = (
            chances * (grad_chances - jnp.sum(grad_chances * chances, -1, keepdims=True))
        ).astype(jnp.bfloat16)
        grad_query = (
            jnp.einsum("eqk,kh->eqh", grad_scores, key_one, preferred_element_type=jnp.float32)
            * scale
        ).astype(jnp.bfloat16)
        grad_key = (
            jnp.einsum("eqk,eqh->kh", grad_scores, query_one, preferred_element_type=jnp.float32)
            * scale
        )
        grad_value = jnp.einsum(
            "eqk,eqh->kh",
            chances.astype(jnp.bfloat16),
            grad_one,
            preferred_element_type=jnp.float32,
        )
        return (grad_query, jnp.concatenate([grad_key, grad_value], 1))

    grad_query, grad_pair = lax.map(
        single, (query_seq, key_seq, value_seq, seq_lengths, sequence_total, grad_seq)
    )
    grad_query = jnp.moveaxis(grad_query, 0, 1).reshape(experts_local, block_rows, head_size)
    return (grad_query, grad_pair.reshape(block_rows, 2 * head_size))


def mixture_forward(
    normed, pair_rows, gate_w, query_w, output_w, routes, seq_lengths, causal, head_index
):
    experts_local = query_w.shape[0]
    head_size = query_w.shape[2]
    logits = jnp.dot(normed, gate_w, preferred_element_type=jnp.float32)
    _, _, grid = gate_parts(logits, routes)
    local_gates = lax.dynamic_slice_in_dim(grid, head_index * experts_local, experts_local, 1)
    queries = jnp.einsum("td,edh->eth", normed, query_w, preferred_element_type=jnp.float32).astype(
        jnp.bfloat16
    )
    attended, log_total = attend(
        queries, pair_rows[:, :head_size], pair_rows[:, head_size:], seq_lengths, causal
    )
    gated = (local_gates.T[:, :, None] * attended).astype(jnp.bfloat16)
    partial_value = jnp.einsum("eth,ehd->td", gated, output_w, preferred_element_type=jnp.float32)
    return (partial_value, attended, log_total)


def mixture_back(
    normed,
    pair_rows,
    gate_w,
    query_w,
    output_w,
    routes,
    seq_lengths,
    causal,
    head_index,
    attended,
    log_total,
    grad_rows,
):
    experts_local = query_w.shape[0]
    head_size = query_w.shape[2]
    local_rows = normed.shape[0] // lax.axis_size("head")
    logits = jnp.dot(normed, gate_w, preferred_element_type=jnp.float32)
    gate_values, onehot, grid = gate_parts(logits, routes)
    local_gates = lax.dynamic_slice_in_dim(grid, head_index * experts_local, experts_local, 1)
    queries = jnp.einsum("td,edh->eth", normed, query_w, preferred_element_type=jnp.float32).astype(
        jnp.bfloat16
    )
    gated = (local_gates.T[:, :, None] * attended).astype(jnp.bfloat16)
    grad_output = jnp.einsum("eth,td->ehd", gated, grad_rows, preferred_element_type=jnp.float32)
    grad_gated = (
        jnp.einsum("td,ehd->eth", grad_rows, output_w, preferred_element_type=jnp.float32)
        .astype(jnp.bfloat16)
        .astype(jnp.float32)
    )
    grad_local = jnp.sum(grad_gated * attended, -1)
    grad_attended = (local_gates.T[:, :, None] * grad_gated).astype(jnp.bfloat16)
    grad_query, grad_pair = attend_back(
        queries,
        pair_rows[:, :head_size],
        pair_rows[:, head_size:],
        seq_lengths,
        causal,
        log_total,
        grad_attended,
    )
    grad_query_w = jnp.einsum("td,eth->edh", normed, grad_query, preferred_element_type=jnp.float32)
    grad_normed = jnp.einsum("eth,edh->td", grad_query, query_w, preferred_element_type=jnp.float32)
    grad_grid = lax.dynamic_update_slice_in_dim(
        jnp.zeros_like(grid), grad_local.T, head_index * experts_local, 1
    )
    total_pair, total_grid = (
        lax.psum(grad_pair.astype(jnp.bfloat16), "head").astype(jnp.float32),
        lax.psum(grad_grid.astype(jnp.bfloat16), "head").astype(jnp.float32),
    )
    grad_logits = gate_back(gate_values, onehot, total_grid)
    own_logits = own_rows(grad_logits, head_index, local_rows)
    own_normed = own_rows(normed, head_index, local_rows).astype(jnp.float32)
    grad_gate_w = jnp.einsum("td,te->de", own_normed, own_logits, precision=PRECISE)
    router_rows = jnp.einsum("te,de->td", own_logits, gate_w.astype(jnp.float32), precision=PRECISE)
    own_pair = own_rows(total_pair, head_index, local_rows).astype(jnp.bfloat16)
    return (grad_normed, router_rows, own_pair, grad_query_w, grad_output, grad_gate_w)


def feed(normed, up_full, down_full):
    hidden = jnp.dot(normed, up_full, preferred_element_type=jnp.float32)
    return jnp.dot(
        gelu_tanh(hidden).astype(jnp.bfloat16), down_full, preferred_element_type=jnp.float32
    )


def feed_back(normed, grad_rows, up_full, down_full):
    hidden = jnp.dot(normed, up_full, preferred_element_type=jnp.float32)
    activated, pull = jax.vjp(gelu_tanh, hidden)
    grad_down = jnp.einsum(
        "tf,td->fd", activated.astype(jnp.bfloat16), grad_rows, preferred_element_type=jnp.float32
    )
    grad_act = jnp.einsum("td,fd->tf", grad_rows, down_full, preferred_element_type=jnp.float32)
    grad_hidden = pull(grad_act)[0].astype(jnp.bfloat16)
    grad_up = jnp.einsum("td,tf->df", normed, grad_hidden, preferred_element_type=jnp.float32)
    grad_normed = jnp.einsum("tf,df->td", grad_hidden, up_full, preferred_element_type=jnp.float32)
    return (grad_up, grad_down, grad_normed)


def on_device(
    tokens,
    self_routes,
    cross_routes,
    lengths,
    cotangent,
    norm_attn,
    norm_ffn,
    norm_final,
    norm_cross,
    router,
    query_weight,
    key_weight,
    value_weight,
    output_weight,
    up_weight,
    down_weight,
    cross_router,
    cross_query,
    cross_key,
    cross_value,
    cross_output,
):
    section_index = lax.axis_index("section")
    head_index = lax.axis_index("head")
    (
        gain_attn,
        gain_ffn,
        gain_final,
        gain_cross,
        gate_self,
        query_self,
        key_self,
        value_self,
        output_self,
        up_full,
        down_full,
        gate_cross,
        query_cross,
        key_across,
        value_across,
        output_cross,
    ) = (
        lax.all_gather(norm_attn, "dp", axis=0, tiled=True),
        lax.all_gather(norm_ffn, "dp", axis=0, tiled=True),
        lax.all_gather(norm_final, "dp", axis=0, tiled=True),
        lax.all_gather(norm_cross, "dp", axis=0, tiled=True),
        lax.all_gather(router, "dp", axis=0, tiled=True),
        lax.all_gather(query_weight, "dp", axis=1, tiled=True),
        lax.all_gather(key_weight, "dp", axis=0, tiled=True),
        lax.all_gather(value_weight, "dp", axis=0, tiled=True),
        lax.all_gather(output_weight, "dp", axis=2, tiled=True),
        lax.all_gather(up_weight, "dp", axis=0, tiled=True),
        lax.all_gather(down_weight, "dp", axis=1, tiled=True),
        lax.all_gather(cross_router, "dp", axis=0, tiled=True),
        lax.all_gather(cross_query, "dp", axis=1, tiled=True),
        lax.all_gather(cross_key, "dp", axis=0, tiled=True),
        lax.all_gather(cross_value, "dp", axis=0, tiled=True),
        lax.all_gather(cross_output, "dp", axis=2, tiled=True),
    )
    span_rows = self_routes.shape[2]
    gain_attn = gain_attn.astype(jnp.float32)
    gain_ffn = gain_ffn.astype(jnp.float32)
    gain_final = gain_final.astype(jnp.float32)
    gain_cross = gain_cross.astype(jnp.float32)
    pair_self = jnp.concatenate([key_self, value_self], 1)
    pair_cross = jnp.concatenate([key_across, value_across], 1)
    micro_count = tokens.shape[1]
    local_rows = tokens.shape[2]
    width = tokens.shape[3]
    block_rows = self_routes.shape[2]
    experts_here = query_self.shape[0]
    head_size = query_self.shape[2]
    decoding = section_index == 1
    decoder_flag = decoding.astype(jnp.float32)
    never = section_index < 0
    own_tokens = tokens[0]
    own_routes = self_routes[0]
    own_lengths = select_at(lengths, section_index)
    source_lengths = lengths[0]
    rows_zero = jnp.zeros((micro_count, local_rows, width), jnp.float32)
    normed_zero = jnp.zeros((micro_count, span_rows, width), jnp.bfloat16)
    pairs_zero = jnp.zeros((micro_count, block_rows, 2 * head_size), jnp.bfloat16)
    attended_zero = jnp.zeros((micro_count, experts_here, span_rows, head_size), jnp.float32)
    totals_zero = jnp.zeros((micro_count, experts_here, span_rows), jnp.float32)
    kept_self_out, kept_cross_out, kept_feed_out = (rows_zero, rows_zero, rows_zero)
    kept_normed_self, kept_normed_cross, saved_normed_feedforward = (
        normed_zero,
        normed_zero,
        normed_zero,
    )
    kept_pairs_self, kept_pairs_cross = (pairs_zero, pairs_zero)
    kept_received = jnp.zeros((micro_count, local_rows, width), jnp.bfloat16)
    kept_attended_self, kept_attended_cross = (attended_zero, attended_zero)
    kept_total_self, kept_total_cross = (totals_zero, totals_zero)
    kept_result = jnp.zeros((micro_count, local_rows, width), jnp.bfloat16)
    received = jnp.zeros((local_rows, width), jnp.bfloat16)
    for counter in range(micro_count + 1):
        position = counter - section_index
        active_flag = (position >= 0) & (position < micro_count)
        position = jnp.clip(position, 0, micro_count - 1)
        inputs = select_at(own_tokens, position).astype(jnp.float32)
        lengths_now = select_at(own_lengths, position)
        cross_lengths = select_at(source_lengths, position)
        routes_now = select_at(own_routes, position)
        cross_now = select_at(cross_routes, position)
        normed_own = layer_norm(inputs, gain_attn).astype(jnp.bfloat16)
        normed_self = spread_rows(normed_own)
        pairs_self_now = jnp.dot(normed_self, pair_self, preferred_element_type=jnp.float32).astype(
            jnp.bfloat16
        )
        partial_value, attended_self, total_self = mixture_forward(
            normed_self,
            pairs_self_now,
            gate_self,
            query_self,
            output_self,
            routes_now,
            lengths_now,
            decoding,
            head_index,
        )
        partial_value = reduce_rows(partial_value)
        after_self = inputs + partial_value
        normed_cross_own = layer_norm(after_self, gain_cross).astype(jnp.bfloat16)
        own_pairs = jnp.dot(received, pair_cross, preferred_element_type=jnp.float32).astype(
            jnp.bfloat16
        )
        normed_cross = spread_rows(normed_cross_own)
        pairs_cross_now = spread_rows(own_pairs)
        partial_value, attended_cross, total_cross = mixture_forward(
            normed_cross,
            pairs_cross_now,
            gate_cross,
            query_cross,
            output_cross,
            cross_now,
            cross_lengths,
            never,
            head_index,
        )
        partial_value = reduce_rows(partial_value)
        after_cross = after_self + decoder_flag * partial_value
        normed_feed_own = layer_norm(after_cross, gain_ffn).astype(jnp.bfloat16)
        normed_feed = spread_rows(normed_feed_own)
        partial_value = reduce_rows(feed(normed_feed, up_full, down_full))
        after_feedforward = after_cross + partial_value
        memory = layer_norm(after_feedforward, gain_final).astype(jnp.bfloat16)
        result = jnp.where(decoding, after_feedforward.astype(jnp.bfloat16), memory)
        kept_self_out = keep_at(kept_self_out, position, after_self, active_flag)
        kept_cross_out = keep_at(kept_cross_out, position, after_cross, active_flag)
        kept_feed_out = keep_at(kept_feed_out, position, after_feedforward, active_flag)
        kept_normed_self = keep_at(kept_normed_self, position, normed_self, active_flag)
        kept_normed_cross = keep_at(kept_normed_cross, position, normed_cross, active_flag)
        saved_normed_feedforward = keep_at(
            saved_normed_feedforward, position, normed_feed, active_flag
        )
        kept_pairs_self = keep_at(kept_pairs_self, position, pairs_self_now, active_flag)
        kept_pairs_cross = keep_at(kept_pairs_cross, position, pairs_cross_now, active_flag)
        kept_received = keep_at(kept_received, position, received, active_flag)
        kept_attended_self = keep_at(kept_attended_self, position, attended_self, active_flag)
        kept_attended_cross = keep_at(kept_attended_cross, position, attended_cross, active_flag)
        kept_total_self = keep_at(kept_total_self, position, total_self, active_flag)
        kept_total_cross = keep_at(kept_total_cross, position, total_cross, active_flag)
        kept_result = keep_at(kept_result, position, result, active_flag)
        received = shifted(memory, "section", 1)
    vector_zero = jnp.zeros(gain_attn.shape, jnp.float32)
    acc_attn, acc_ffn, acc_final, acc_cross = (vector_zero, vector_zero, vector_zero, vector_zero)
    acc_gate_self = jnp.zeros(gate_self.shape, jnp.float32)
    acc_query_self = jnp.zeros(query_self.shape, jnp.float32)
    acc_pair_self = jnp.zeros(pair_self.shape, jnp.float32)
    acc_output_self = jnp.zeros(output_self.shape, jnp.float32)
    acc_up = jnp.zeros(up_full.shape, jnp.float32)
    acc_down = jnp.zeros(down_full.shape, jnp.float32)
    acc_gate_cross = jnp.zeros(gate_cross.shape, jnp.float32)
    acc_query_cross = jnp.zeros(query_cross.shape, jnp.float32)
    acc_pair_cross = jnp.zeros(pair_cross.shape, jnp.float32)
    acc_output_cross = jnp.zeros(output_cross.shape, jnp.float32)
    input_grads = rows_zero
    back_received = jnp.zeros((local_rows, width), jnp.bfloat16)
    for counter in range(micro_count + 1):
        position = counter - 1 + section_index
        active_flag = (position >= 0) & (position < micro_count)
        position = jnp.clip(position, 0, micro_count - 1)
        alive_marker = active_flag.astype(jnp.float32)
        inputs = select_at(own_tokens, position).astype(jnp.float32)
        after_self = select_at(kept_self_out, position)
        after_cross = select_at(kept_cross_out, position)
        after_feedforward = select_at(kept_feed_out, position)
        normed_self = select_at(kept_normed_self, position)
        normed_cross = select_at(kept_normed_cross, position)
        normed_feed = select_at(saved_normed_feedforward, position)
        pairs_self_now = select_at(kept_pairs_self, position)
        pairs_cross_now = select_at(kept_pairs_cross, position)
        source_own = select_at(kept_received, position)
        result = select_at(kept_result, position)
        lengths_now = select_at(own_lengths, position)
        cross_lengths = select_at(source_lengths, position)
        routes_now = select_at(own_routes, position)
        cross_now = select_at(cross_routes, position)
        grad_memory = back_received.astype(jnp.float32)
        from_memory, grad_gain = norm_back(after_feedforward, gain_final, grad_memory)
        acc_final = acc_final + grad_gain
        grad_top = (
            jnp.where(decoding, select_at(cotangent, position).astype(jnp.float32), from_memory)
            * alive_marker
        )
        grad_up, grad_down, partial_value = feed_back(
            normed_feed, spread_grads(grad_top.astype(jnp.bfloat16)), up_full, down_full
        )
        grad_into = reduce_grads(partial_value)
        acc_up = acc_up + grad_up
        acc_down = acc_down + grad_down
        into_norm, grad_gain = norm_back(after_cross, gain_ffn, grad_into)
        acc_ffn = acc_ffn + grad_gain
        grad_cross_out = grad_top + into_norm
        grad_low = (grad_cross_out * decoder_flag).astype(jnp.bfloat16)
        partial_value, router_rows, pair_rows, grad_query, grad_output, grad_gate = mixture_back(
            normed_cross,
            pairs_cross_now,
            gate_cross,
            query_cross,
            output_cross,
            cross_now,
            cross_lengths,
            never,
            head_index,
            select_at(kept_attended_cross, position),
            select_at(kept_total_cross, position),
            spread_grads(grad_low),
        )
        grad_normed = reduce_grads(partial_value) + router_rows
        acc_query_cross = acc_query_cross + grad_query
        acc_output_cross = acc_output_cross + grad_output
        acc_gate_cross = acc_gate_cross + grad_gate
        outgoing = jnp.dot(pair_rows, pair_cross.T, preferred_element_type=jnp.float32).astype(
            jnp.bfloat16
        )
        acc_pair_cross = acc_pair_cross + jnp.einsum(
            "td,tc->dc", source_own, pair_rows, preferred_element_type=jnp.float32
        )
        into_norm, grad_gain = norm_back(after_self, gain_cross, grad_normed)
        acc_cross = acc_cross + grad_gain
        grad_self_out = grad_cross_out + into_norm
        grad_low = grad_self_out.astype(jnp.bfloat16)
        partial_value, router_rows, pair_rows, grad_query, grad_output, grad_gate = mixture_back(
            normed_self,
            pairs_self_now,
            gate_self,
            query_self,
            output_self,
            routes_now,
            lengths_now,
            decoding,
            head_index,
            select_at(kept_attended_self, position),
            select_at(kept_total_self, position),
            spread_grads(grad_low),
        )
        grad_normed = reduce_grads(partial_value) + router_rows
        normed_mine = own_rows(normed_self, head_index, local_rows)
        acc_query_self = acc_query_self + grad_query
        acc_output_self = acc_output_self + grad_output
        acc_gate_self = acc_gate_self + grad_gate
        acc_pair_self = acc_pair_self + jnp.einsum(
            "td,tc->dc", normed_mine, pair_rows, preferred_element_type=jnp.float32
        )
        grad_normed = grad_normed + jnp.dot(
            pair_rows, pair_self.T, preferred_element_type=jnp.float32
        )
        into_norm, grad_gain = norm_back(inputs, gain_attn, grad_normed)
        acc_attn = acc_attn + grad_gain
        input_grads = keep_at(input_grads, position, grad_self_out + into_norm, active_flag)
        back_received = shifted(outgoing, "section", -1)
    scattered = (
        summed_on_arrival(acc_attn.astype(jnp.bfloat16), "dp", 0),
        summed_on_arrival(acc_ffn.astype(jnp.bfloat16), "dp", 0),
        summed_on_arrival(acc_final.astype(jnp.bfloat16), "dp", 0),
        *sent_together(
            (acc_cross.astype(jnp.bfloat16), acc_gate_self.astype(jnp.bfloat16)), "dp", 0, 1
        ),
        summed_on_arrival(acc_query_self.astype(jnp.bfloat16), "dp", 1),
        *side_by_side(
            (
                acc_pair_self[:, :head_size].astype(jnp.bfloat16),
                acc_pair_self[:, head_size:].astype(jnp.bfloat16),
            ),
            "dp",
            0,
            1,
        ),
        summed_on_arrival(acc_output_self.astype(jnp.bfloat16), "dp", 2),
        summed_on_arrival(acc_up.astype(jnp.bfloat16), "dp", 0),
        summed_on_arrival(acc_down.astype(jnp.bfloat16), "dp", 1),
        summed_on_arrival(acc_gate_cross.astype(jnp.bfloat16), "dp", 0),
        summed_on_arrival(acc_query_cross.astype(jnp.bfloat16), "dp", 1),
        *side_by_side(
            (
                acc_pair_cross[:, :head_size].astype(jnp.bfloat16),
                acc_pair_cross[:, head_size:].astype(jnp.bfloat16),
            ),
            "dp",
            0,
            1,
        ),
        summed_on_arrival(acc_output_cross.astype(jnp.bfloat16), "dp", 2),
    )
    split_sums = (
        lax.psum(scattered[5].astype(jnp.bfloat16), "section").astype(jnp.float32),
        lax.psum(scattered[8].astype(jnp.bfloat16), "section").astype(jnp.float32),
        lax.psum(scattered[9].astype(jnp.bfloat16), "section").astype(jnp.float32),
        lax.psum(scattered[10].astype(jnp.bfloat16), "section").astype(jnp.float32),
        lax.psum(scattered[12].astype(jnp.bfloat16), "section").astype(jnp.float32),
        lax.psum(scattered[15].astype(jnp.bfloat16), "section").astype(jnp.float32),
    )
    shared_sums = lax.psum(
        (
            scattered[0],
            scattered[1],
            scattered[2],
            scattered[3],
            scattered[4],
            scattered[6],
            scattered[7],
            scattered[11],
            scattered[13],
            scattered[14],
        ),
        ("section", "head"),
    )
    return (
        kept_result[None],
        input_grads[None],
        shared_sums[0],
        shared_sums[1],
        shared_sums[2],
        shared_sums[3],
        shared_sums[4],
        split_sums[0],
        shared_sums[5],
        shared_sums[6],
        split_sums[1],
        split_sums[2],
        split_sums[3],
        shared_sums[7],
        split_sums[4],
        shared_sums[8],
        shared_sums[9],
        split_sums[5],
    )


def solution(mesh):
    return jax.shard_map(
        on_device,
        mesh=mesh,
        in_specs=(
            P("section", None, ("dp", "head"), None),
            P("section", None, "dp", None),
            P(None, "dp", None),
            P(None, None, "dp"),
            P(None, ("dp", "head"), None),
            P("dp"),
            P("dp"),
            P("dp"),
            P("dp"),
            P("dp", None),
            P("head", "dp", None),
            P("dp", None),
            P("dp", None),
            P("head", None, "dp"),
            P("dp", "head"),
            P("head", "dp"),
            P("dp", None),
            P("head", "dp", None),
            P("dp", None),
            P("dp", None),
            P("head", None, "dp"),
        ),
        out_specs=(
            P("section", None, ("dp", "head"), None),
            P("section", None, ("dp", "head"), None),
            P("dp"),
            P("dp"),
            P("dp"),
            P("dp"),
            P("dp", None),
            P("head", "dp", None),
            P("dp", None),
            P("dp", None),
            P("head", None, "dp"),
            P("dp", "head"),
            P("head", "dp"),
            P("dp", None),
            P("head", "dp", None),
            P("dp", None),
            P("dp", None),
            P("head", None, "dp"),
        ),
        check_vma=False,
    )
```

profile of v0, /device:TPU:0, one launch (start us, length us, event | category | flops | bytes accessed | tf_op | source)
XLA Modules:
  0.0 1525.8 jit_solution(4579051863566533992)
XLA Ops:
  17.9 18.6 %all-reduce.5 = (bf16[512]{0:T(512)(128)(2,1)S(1)}, bf16[512]{0:T(512)(128)(2,1)}, bf16[512]{0:T(512)(128)(2,1)}, bf16[512]{0:T(512)(128)(2,1)}) all-reduce(bf16[512]{0:T(512)(128)(2,1)S(1)} %dynamic-update-slice, bf16[512]{0:T(512)(128)(2,1)S(1)} %dynamic-update-slice.3, ...), channel_id=1, replica_groups=mesh['section'=2,'dp'=8,'head'=2] {'dp'}, use_global_device_ids=true, to_apply=%add | all-reduce | flops 2048 | bytes 8192
  38.8 14.2 all_gather.114
  62.1 14.2 all_gather.117
  77.2 14.0 all_gather.115
  91.1 14.0 all_gather.116
  118.8 19.8 %reduce-scatter.31.cloned.1.call-done = bf16[512,512]{1,0:T(8,128)(2,1)} async-done(((bf16[1024,512]{1,0:T(8,128)(2,1)}), bf16[512,512]{1,0:T(8,128)(2,1)}) %reduce-scatter.31.cloned.1.call-update) | async-done | bytes 524304 | tf_op jit(solution)/shard_map/reduce_scatter | solution.py:120
  145.8 17.9 %all-gather.33.cloned.1.call-done = bf16[1024,512]{1,0:T(8,128)(2,1)} async-done(((bf16[512,512]{1,0:T(8,128)(2,1)}), bf16[1024,512]{1,0:T(8,128)(2,1)}) %all-gather.33.cloned.1.call-update) | async-done | bytes 1048592 | tf_op jit(solution)/shard_map/all_gather | solution.py:116
  166.1 20.5 %all-gather.23.cloned.1.call-done = bf16[1024,512]{1,0:T(8,128)(2,1)} async-done(((bf16[512,512]{1,0:T(8,128)(2,1)}), bf16[1024,512]{1,0:T(8,128)(2,1)}) %all-gather.23.cloned.1.call-update) | async-done | bytes 1048592 | tf_op jit(solution)/shard_map/all_gather | solution.py:116
  210.5 15.3 %all_gather.121 = bf16[2,512,64]{2,0,1:T(2,128)(2,1)} all-gather(bf16[2,64,64]{2,0,1:T(2,128)(2,1)S(1)} %copy.399), channel_id=1, replica_groups=mesh['section'=2,'dp'=8,'head'=2] {'dp'}, dimensions={1}, use_global_device_ids=true | all-gather | bytes 147456 | tf_op jit(solution)/shard_map/all_gather | solution.py:361
  227.4 23.0 %reduce-scatter.19.cloned.1.call-done = bf16[512,512]{1,0:T(8,128)(2,1)} async-done(((bf16[1024,512]{1,0:T(8,128)(2,1)}), bf16[512,512]{1,0:T(8,128)(2,1)}) %reduce-scatter.19.cloned.1.call-update) | async-done | bytes 524304 | tf_op jit(solution)/shard_map/reduce_scatter | solution.py:120
  256.2 14.3 all_gather.125
  270.5 11.7 all-gather.1
  283.2 13.9 all_gather.122
  297.2 14.0 all_gather.123
  334.5 16.2 %reduce-scatter.21.cloned.1.call-done = bf16[512,512]{1,0:T(8,128)(2,1)} async-done(((bf16[1024,512]{1,0:T(8,128)(2,1)}), bf16[512,512]{1,0:T(8,128)(2,1)}) %reduce-scatter.21.cloned.1.call-update) | async-done | bytes 524304 | tf_op jit(solution)/shard_map/reduce_scatter | solution.py:120
  356.9 20.5 %all-gather.31.cloned.1.call-done = bf16[1024,512]{0,1:T(8,128)(2,1)} async-done(((bf16[1024,64]{0,1:T(8,128)(2,1)}), bf16[1024,512]{0,1:T(8,128)(2,1)}) %all-gather.31.cloned.1.call-update) | async-done | bytes 1048592 | tf_op jit(solution)/shard_map/all_gather | solution.py:359
  377.4 22.2 %all-gather.27.cloned.1.call-done = bf16[1024,512]{1,0:T(8,128)(2,1)} async-done(((bf16[512,512]{1,0:T(8,128)(2,1)}), bf16[1024,512]{1,0:T(8,128)(2,1)}) %all-gather.27.cloned.1.call-update) | async-done | bytes 1048592 | tf_op jit(solution)/shard_map/all_gather | solution.py:116
  407.0 15.3 %all-gather.35.cloned.1.call-done = bf16[1024,512]{1,0:T(8,128)(2,1)} async-done(((bf16[512,512]{1,0:T(8,128)(2,1)}), bf16[1024,512]{1,0:T(8,128)(2,1)}) %all-gather.35.cloned.1.call-update) | async-done | bytes 1048592 | tf_op jit(solution)/shard_map/all_gather | solution.py:116
  424.7 20.2 %reduce-scatter.23.cloned.1.call-done = bf16[512,512]{1,0:T(8,128)(2,1)} async-done(((bf16[1024,512]{1,0:T(8,128)(2,1)}), bf16[512,512]{1,0:T(8,128)(2,1)}) %reduce-scatter.23.cloned.1.call-update) | async-done | bytes 524304 | tf_op jit(solution)/shard_map/reduce_scatter | solution.py:120
  484.3 15.8 %reduce-scatter.27.cloned.1.call-done = bf16[512,512]{1,0:T(8,128)(2,1)} async-done(((bf16[1024,512]{1,0:T(8,128)(2,1)}), bf16[512,512]{1,0:T(8,128)(2,1)}) %reduce-scatter.27.cloned.1.call-update) | async-done | bytes 524304 | tf_op jit(solution)/shard_map/reduce_scatter | solution.py:120
  515.4 12.5 all-gather.37.cloned.1.call-done
  556.8 16.1 %reduce-scatter.29.cloned.1.call-done = bf16[512,512]{1,0:T(8,128)(2,1)} async-done(((bf16[1024,512]{1,0:T(8,128)(2,1)}), bf16[512,512]{1,0:T(8,128)(2,1)}) %reduce-scatter.29.cloned.1.call-update) | async-done | bytes 524304 | tf_op jit(solution)/shard_map/reduce_scatter | solution.py:120
  637.3 16.3 %all-gather.43.cloned.1.call-done = bf16[1024,512]{1,0:T(8,128)(2,1)} async-done(((bf16[512,512]{1,0:T(8,128)(2,1)}), bf16[1024,512]{1,0:T(8,128)(2,1)}) %all-gather.43.cloned.1.call-update) | async-done | bytes 1048592 | tf_op jit(solution)/shard_map/all_gather | solution.py:116
  668.0 11.4 reduce-scatter.35.cloned.1.call-done
  789.2 21.7 %all-reduce.18.cloned.1.call-done = bf16[1024,128]{0,1:T(8,128)(2,1)} async-done(((bf16[1024,128]{0,1:T(8,128)(2,1)}), bf16[1024,128]{0,1:T(8,128)(2,1)}) %all-reduce.18.cloned.1.call-update) | async-done | bytes 262160 | tf_op jit(solution)/shard_map/psum | solution.py:274
  842.8 11.8 all-gather.51.cloned.1.call-done
  903.0 11.2 all-gather.53.cloned.1.call-done
  934.3 21.0 %all-reduce.20.cloned.1.call-done = bf16[1024,128]{0,1:T(8,128)(2,1)} async-done(((bf16[1024,128]{0,1:T(8,128)(2,1)}), bf16[1024,128]{0,1:T(8,128)(2,1)}) %all-reduce.20.cloned.1.call-update) | async-done | bytes 262160 | tf_op jit(solution)/shard_map/psum | solution.py:274
  960.7 11.1 collective-permute-done.3
  1101.3 14.3 reduce-scatter.51.cloned.1.call-done
  1161.4 11.2 all-to-all-done.7
  1462.6 43.0 %all-reduce.22.cloned.1.call-done = (f32[64]{0:T(128)}, f32[64]{0:T(128)}, f32[64]{0:T(128)}, f32[64]{0:T(128)}, f32[64,4]{0,1:T(4,128)}, /*index=5*/f32[64,64]{...) async-done(((f32[64]{0:T(128)}, f32[64]{0:T(128)}, f32[64]{0:T(128)}, f32[64]{0:T(128)}, f32[64,4]{0,1:T(4,128)}, ...) | async-done | bytes 68624 | tf_op jit(solution)/shard_map/psum | solution.py:621
  (1315 shorter events, 966.8 us)
Async XLA Ops:
  8.1 98.8 %all-gather.39.cloned.1.call-start = ((), (), s32[]{:S(2)}) async-start(), calls=%async_computation.45 | async-start | bytes 1572864 | tf_op jit(solution)/shard_map/all_gather | solution.py:116
  38.6 100.0 %reduce-scatter.31.cloned.1.call-start = ((), (), s32[]{:S(2)}) async-start(), calls=%async_computation.46 | async-start | bytes 1572864 | tf_op jit(solution)/shard_map/reduce_scatter | solution.py:120
  145.0 82.4 %reduce-scatter.25.cloned.1.call-start = ((), (), s32[]{:S(2)}) async-start(), calls=%async_computation.40 | async-start | bytes 1572864 | tf_op jit(solution)/shard_map/reduce_scatter | solution.py:120
  210.3 109.4 %all-gather.25.cloned.1.call-start = ((), (), s32[]{:S(2)}) async-start(), calls=%async_computation.33 | async-start | bytes 1572864 | tf_op jit(solution)/shard_map/all_gather | solution.py:116
  256.1 94.5 %reduce-scatter.21.cloned.1.call-start = ((), (), s32[]{:S(2)}) async-start(), calls=%async_computation.34 | async-start | bytes 1572864 | tf_op jit(solution)/shard_map/reduce_scatter | solution.py:120
  334.2 65.4 %all-gather.27.cloned.1.call-start = ((), (), s32[]{:S(2)}) async-start(), calls=%async_computation.35 | async-start | bytes 1572864 | tf_op jit(solution)/shard_map/all_gather | solution.py:116
  356.1 66.3 %all-gather.35.cloned.1.call-start = ((), (), s32[]{:S(2)}) async-start(), calls=%async_computation.41 | async-start | bytes 1572864 | tf_op jit(solution)/shard_map/all_gather | solution.py:116
  356.8 88.0 %reduce-scatter.23.cloned.1.call-start = ((), (), s32[]{:S(2)}) async-start(), calls=%async_computation.38 | async-start | bytes 1572864 | tf_op jit(solution)/shard_map/reduce_scatter | solution.py:120
  405.0 95.1 %reduce-scatter.27.cloned.1.call-start = ((), (), s32[]{:S(2)}) async-start(), calls=%async_computation.42 | async-start | bytes 1572864 | tf_op jit(solution)/shard_map/reduce_scatter | solution.py:120
  511.5 61.3 %reduce-scatter.29.cloned.1.call-start = ((), (), s32[]{:S(2)}) async-start(), calls=%async_computation.44 | async-start | bytes 1572864 | tf_op jit(solution)/shard_map/reduce_scatter | solution.py:120
  533.3 93.8 %reduce-scatter.33.cloned.1.call-start = ((), (), s32[]{:S(2)}) async-start(), calls=%async_computation.48 | async-start | bytes 1572864 | tf_op jit(solution)/shard_map/reduce_scatter | solution.py:120
  658.9 52.2 %all-gather.45.cloned.1.call-start = ((), (), s32[]{:S(2)}) async-start(), calls=%async_computation.51 | async-start | bytes 1572864 | tf_op jit(solution)/shard_map/all_gather | solution.py:126
  689.8 51.4 %reduce-scatter.37.cloned.1.call-start = ((), (), s32[]{:S(2)}) async-start(), calls=%async_computation.52 | async-start | bytes 1572864 | tf_op jit(solution)/shard_map/reduce_scatter | solution.py:130
  748.4 62.6 %all-reduce.18.cloned.1.call-start = ((), (), s32[]{:S(2)}) async-start(), calls=%async_computation.57 | async-start | bytes 524288 | tf_op jit(solution)/shard_map/psum | solution.py:274
  787.6 67.1 %all-gather.51.cloned.1.call-start = ((), (), s32[]{:S(2)}) async-start(), calls=%async_computation.58 | async-start | bytes 1572864 | tf_op jit(solution)/shard_map/all_gather | solution.py:126
  892.7 62.6 %all-reduce.20.cloned.1.call-start = ((), (), s32[]{:S(2)}) async-start(), calls=%async_computation.64 | async-start | bytes 524288 | tf_op jit(solution)/shard_map/psum | solution.py:274
  932.0 66.5 %all-gather.57.cloned.1.call-start = ((), (), s32[]{:S(2)}) async-start(), calls=%async_computation.65 | async-start | bytes 1572864 | tf_op jit(solution)/shard_map/all_gather | solution.py:126
  978.1 50.8 %reduce-scatter.49.cloned.1.call-start = ((), (), s32[]{:S(2)}) async-start(), calls=%async_computation.66 | async-start | bytes 1572864 | tf_op jit(solution)/shard_map/reduce_scatter | solution.py:130
  1036.5 59.5 %reduce-scatter.39.cloned.1.call-start = ((), (), s32[]{:S(2)}) async-start(), calls=%async_computation.54 | async-start | bytes 1572864 | tf_op jit(solution)/shard_map/reduce_scatter | solution.py:130
  1044.5 54.1 %reduce-scatter.45.cloned.1.call-start = ((), (), s32[]{:S(2)}) async-start(), calls=%async_computation.61 | async-start | bytes 1572864 | tf_op jit(solution)/shard_map/reduce_scatter | solution.py:130
  1056.9 58.7 %reduce-scatter.51.cloned.1.call-start = ((), (), s32[]{:S(2)}) async-start(), calls=%async_computation.68 | async-start | bytes 1572864 | tf_op jit(solution)/shard_map/reduce_scatter | solution.py:130
  1090.5 50.8 %all-to-all-start.8 = ((bf16[8,1024,64]{1,2,0:T(8,128)(2,1)}), bf16[8,1024,64]{1,2,0:T(8,128)(2,1)}, u32[]{:S(2)}, u32[]{:S(2)}) async-start(bf16[8,1024,64]{1,2,0:T(8,128)(2,1)} %bitcast.1286), calls=%async_computation.26 | async-start | bytes 2097152 | tf_op jit(solution)/shard_map/all_to_all | solution.py:26
  1095.4 109.8 %all-gather.55.cloned.1.call-start = ((), (), s32[]{:S(2)}) async-start(), calls=%async_computation.62 | async-start | bytes 1572864 | tf_op jit(solution)/shard_map/all_gather | solution.py:126
  1124.9 82.8 %all-gather.49.cloned.1.call-start = ((), (), s32[]{:S(2)}) async-start(), calls=%async_computation.55 | async-start | bytes 1572864 | tf_op jit(solution)/shard_map/all_gather | solution.py:126
  1146.0 64.3 %all-gather.61.cloned.1.call-start = ((), (), s32[]{:S(2)}) async-start(), calls=%async_computation.69 | async-start | bytes 1572864 | tf_op jit(solution)/shard_map/all_gather | solution.py:126
  1150.7 214.5 %all-reduce.28.cloned.1.call-start = ((), (), s32[]{:S(2)}) async-start(), calls=%async_computation.74 | async-start | bytes 524288 | tf_op jit(solution)/shard_map/psum | solution.py:616
  1193.5 105.3 %all-to-all-start.12 = ((bf16[8,2,4096]{2,1,0:T(2,128)(2,1)}), bf16[8,2,4096]{2,1,0:T(2,128)(2,1)}, u32[]{:S(2)}, u32[]{:S(2)}) async-start(bf16[8,2,4096]{2,1,0:T(2,128)(2,1)} %reshape.2346), calls=%async_computation.30 | async-start | bytes 262144 | tf_op jit(solution)/shard_map/all_to_all | solution.py:26
  1197.5 213.9 %all-reduce.24.cloned.1.call-start = ((), (), s32[]{:S(2)}) async-start(), calls=%async_computation.72 | async-start | bytes 2097152 | tf_op jit(solution)/shard_map/psum | solution.py:274
  1326.0 102.1 %all-reduce.26.cloned.1.call-start = ((), (), s32[]{:S(2)}) async-start(), calls=%async_computation.73 | async-start | bytes 262144 | tf_op jit(solution)/shard_map/psum | solution.py:614
  1344.7 90.6 %reduce-scatter.47.cloned.1.call-start = ((), (), s32[]{:S(2)}) async-start(), calls=%async_computation.63 | async-start | bytes 1572864 | tf_op jit(solution)/shard_map/reduce_scatter | solution.py:130
  1359.2 77.9 %reduce-scatter.41.cloned.1.call-start = ((), (), s32[]{:S(2)}) async-start(), calls=%async_computation.56 | async-start | bytes 1572864 | tf_op jit(solution)/shard_map/reduce_scatter | solution.py:130
  1453.4 52.2 %all-reduce.22.cloned.1.call-start = ((), (), s32[]{:S(2)}) async-start(), calls=%async_computation.71 | async-start | bytes 274432 | tf_op jit(solution)/shard_map/psum | solution.py:621
  (316 other events, 5856.3 us)
Sparse Core Ops, SparseCore 0:
  38.7 19.5 all-gather.38
  118.9 19.6 reduce-scatter.30
  142.4 21.3 all-gather.32
  165.2 21.2 all-gather.22
  207.1 20.3 reduce-scatter.24
  230.1 20.3 reduce-scatter.18
  256.3 21.2 all-gather.24
  333.1 17.4 reduce-scatter.20
  605.7 21.3 reduce-scatter.32
  659.0 20.3 reduce-scatter.34
  748.5 21.2 all-gather.46
  787.7 23.1 all-reduce.17
  834.2 20.3 all-gather.50
  892.9 21.2 all-gather.52
  932.1 23.1 all-reduce.19
  1008.5 20.3 reduce-scatter.48
  1044.6 25.7 reduce-scatter.38
  1072.6 20.3 reduce-scatter.44
  1095.2 20.3 reduce-scatter.50
  1459.7 45.8 all-reduce.21
Sparse Core Ops, SparseCore 1:
  335.1 19.1 all-gather.28
  355.7 21.6 all-gather.30
  378.8 20.7 all-gather.26
  401.2 21.1 all-gather.34
  424.6 20.2 reduce-scatter.22
  478.8 21.2 reduce-scatter.26
  506.7 21.1 all-gather.36
  529.3 21.1 all-gather.40
  552.6 20.2 reduce-scatter.28
  632.4 21.1 all-gather.42
  689.9 21.1 all-gather.44
  721.0 20.2 reduce-scatter.36
  864.6 20.2 reduce-scatter.42
  978.2 20.3 all-gather.56
  1036.5 21.4 all-gather.58
  1125.0 21.2 all-gather.54
  1147.8 21.1 all-gather.48
  1170.6 21.1 all-gather.60
  1194.1 23.0 all-reduce.27
  1289.0 41.7 all-reduce.23
  1344.8 22.9 all-reduce.25
  1369.9 20.2 reduce-scatter.46
  1392.9 20.2 reduce-scatter.40
  1415.5 20.2 reduce-scatter.52
where the time goes:
time: 1540 us; the launch traced here: 1530 us
  waiting for transfers between devices  509 us (33%)
  matrix products  352 us (23%)
  other arithmetic  254 us (16%)
  blocking collectives  186 us (12%)
  local copies, waits for them, and re-layouts  133 us (9%)
  starting transfers between devices  70.4 us (5%)
  between operations  21.9 us (1%)
    reduce_scatter x9, waiting for transfers between devices, reduce_rows(): lax.psum_scatter(partial_value.astype(jnp.bfloat16), 'head', scatter_dime...  134 us
    all_gather x9, waiting for transfers between devices, spread_rows(): return lax.all_gather(rows, 'head', axis=0, tiled=True)  112 us
    unnamed x613, local copies, waits for them, and re-layouts  77.1 us
    all_to_all x13, starting transfers between devices, summed_on_arrival(): lax.all_to_all(blocks, axis, split_axis=0, concat_axis=0, tiled=True)  55.8 us
    all_gather x9, waiting for transfers between devices, spread_grads(): return lax.all_gather(rows, 'head', axis=0, tiled=True)  55 us
    dynamic_update_slice x35, other arithmetic, keep_at(): lax.dynamic_update_index_in_dim(table, jnp.where(active_flag, value, prev...  47.6 us
    psum x1, waiting for transfers between devices, on_device(): lax.psum((scattered[0], scattered[1], scattered[2], scattered[3], scatter...  43 us
    psum x3, waiting for transfers between devices, mixture_back(): lax.psum(grad_pair.astype(jnp.bfloat16), 'head').astype(jnp.float32)  42.7 us
  transfers between devices with their start and end apart: 61, of which 41 were waited for; matrix products, arithmetic and copies ran while one was open for 31% of the time, Pallas kernels for 0%

commit v1 on v0

v1 whole, which is shorter than its diff:
```python
import functools
import math

import jax
import jax.numpy as jnp
from jax import lax
from jax.experimental import pallas as pl
from jax.experimental.pallas import tpu as pltpu
from jax.sharding import PartitionSpec as P

EPSILON = 1e-05
FAR = -1e30
F32 = jnp.float32
BF16 = jnp.bfloat16
MESH = pl.DeviceIdType.MESH
NN = (((1,), (0,)), ((), ()))
NT = (((1,), (1,)), ((), ()))
TN = (((0,), (0,)), ((), ()))


def mm(a, b, dims=NN):
    return lax.dot_general(a, b, dims, preferred_element_type=F32)


def chunks(total, size, body):
    def step(i, carry):
        body(pl.ds(pl.multiple_of(i * size, size), size))
        return carry

    lax.fori_loop(0, total // size, step, 0)


def norm_parts(x):
    centred = x - jnp.mean(x, -1, keepdims=True)
    rstd = lax.rsqrt(jnp.mean(centred * centred, -1, keepdims=True) + EPSILON)
    return centred * rstd, rstd


def norm_back(x, gain, dz):
    xhat, rstd = norm_parts(x)
    dxh = dz * gain
    dx = (
        dxh
        - jnp.mean(dxh, -1, keepdims=True)
        - xhat * jnp.mean(dxh * xhat, -1, keepdims=True)
    ) * rstd
    return dx, jnp.sum(dz * xhat, 0, keepdims=True)


class Rows:
    def __init__(self, q, h):
        at = 0
        for name, size in (
            ("q", q), ("kv", 2 * h), ("r", 16), ("o", q),
            ("cq", q), ("cr", 16), ("ckv", 2 * h), ("co", q), ("gain", 16),
        ):
            setattr(self, name, slice(at, at + size))
            at += size
        self.total = at
        self.self_in = slice(self.q.start, self.r.stop)
        self.cross_in = slice(self.cq.start, self.cr.stop)


def layer_kernel(
    rows, experts, hs,
    src_ref, tgt_ref, mask_ref, lens_ref, ct_ref, wa_ref, up_ref, down_ref,
    mem_ref, y_ref, dsrc_ref, dtgt_ref, ga_ref, gup_ref, gdown_ref,
    a1, qT, kvT, kT, vT, kA, vA, qA, dA, gate, prob, attT, rl, hT, dT, dkv,
    mid, top, fa, b2, act, gp, work, workb, gacc, kvs, kvr, send_sem, recv_sem,
):
    R, W = src_ref.shape
    T = 2 * R
    FF = up_ref.shape[1]
    QR = experts * hs
    half = lax.axis_index("head")
    peer = {"head": 1 - half}
    LC = 128
    FC = 512
    scale = 1.0 / math.sqrt(hs)
    ENC, DEC, CROSS = 0, 1, 2

    barrier = pltpu.get_barrier_semaphore()
    pl.semaphore_signal(barrier, inc=1, device_id=peer, device_id_type=MESH)
    pl.semaphore_wait(barrier, 1)

    def exchange(slot):
        return pltpu.make_async_remote_copy(
            src_ref=kvs.at[slot], dst_ref=kvr.at[slot],
            send_sem=send_sem.at[slot], recv_sem=recv_sem.at[slot],
            device_id=peer, device_id_type=MESH,
        )

    def gain(k):
        at = rows.gain.start
        return wa_ref[at : at + 16, :].astype(F32)[k : k + 1, :]

    gacc[...] = jnp.zeros_like(gacc)

    def norm_to(source, out, base, k):
        g = gain(k)

        def body(s):
            xhat, _ = norm_parts(source[s, :].astype(F32))
            out[pl.ds(base + s.start, LC), :] = (xhat * g).astype(BF16)

        chunks(R, LC, body)

    def gates(m, logits):
        named = mask_ref[8 * m : 8 * m + experts, :]
        l = jnp.where(named > 0, logits[0:experts], FAR)
        p = jnp.exp(l - jnp.max(l, 0, keepdims=True)) * named
        gate[m, 0:experts, :] = p / jnp.sum(p, 0, keepdims=True)

    def set_keys(m, length_row):
        lane = lax.broadcasted_iota(jnp.int32, (1, T), 1)
        pos = jnp.where(lane < R, lane + half * R, lane - R + (1 - half) * R).astype(F32)
        length = lens_ref[length_row : length_row + 1, 0:1]
        outside = jnp.where(pos < length, 0.0, FAR)
        kT[m, 0:hs, :] = kvT[m, 0:hs, :]
        sub = lax.broadcasted_iota(jnp.int32, (128 - hs, T), 0)
        kT[m, hs:128, :] = jnp.where(sub == 0, outside, 0.0).astype(BF16)
        vT[m, 0:hs, :] = kvT[m, hs : 2 * hs, :]
        vT[m, hs:128, :] = jnp.where(sub < 2, 1.0, 0.0).astype(BF16)
        kA[m] = kT[m].astype(F32).T.astype(BF16)
        vA[m] = vT[m].astype(F32).T.astype(BF16)

    sub = lax.broadcasted_iota(jnp.int32, (128 - hs, R), 0)
    qA[hs:128, :] = jnp.where(sub == 0, 1.0, 0.0).astype(BF16)
    dA[hs:128, :] = jnp.zeros((128 - hs, R), BF16)

    def attend(m, causal):
        def one(e, carry):
            qA[0:hs, :] = qT[m, e]
            scores = mm(kA[m], qA[...])
            if causal:
                k = lax.broadcasted_iota(jnp.int32, (T, 1), 0)
                k = jnp.where(k < R, k + half * R, k - R + (1 - half) * R)
                q = lax.broadcasted_iota(jnp.int32, (1, R), 1) + half * R
                scores = jnp.where(k <= q, scores, FAR)
            p = jnp.exp(scores - jnp.max(scores, 0, keepdims=True)).astype(BF16)
            prob[m, e] = p
            out = mm(vT[m, 0 : hs + 16, :], p)
            inverse = 1.0 / out[hs : hs + 1, :]
            attended = out[0:hs, :] * inverse
            attT[m, e] = attended
            rl[m, pl.ds(e, 1), :] = inverse
            hT[m, pl.ds(pl.multiple_of(e * hs, hs), hs), :] = (
                gate[m, pl.ds(e, 1), :] * attended
            ).astype(BF16)
            return carry

        lax.fori_loop(0, experts, one, 0)

    def attend_back(m, dout, wo):
        dH = mm(wa_ref[wo, :], dout, NT).astype(BF16)
        ga = mm(hT[m], dout)
        work[0:QR, :] = dH.astype(F32)
        dkv[...] = jnp.zeros_like(dkv)

        def one(e, carry):
            d = work[pl.ds(pl.multiple_of(e * hs, hs), hs), 0:R]
            dg = jnp.sum(d * attT[m, e], 0, keepdims=True)
            g = gate[m, pl.ds(e, 1), :]
            inverse = rl[m, pl.ds(e, 1), :]
            gate[m, pl.ds(experts + e, 1), :] = dg
            da = (d * (g * inverse)).astype(BF16)
            delta = g * dg * inverse
            high = delta.astype(BF16).astype(F32)
            row = lax.broadcasted_iota(jnp.int32, (16, R), 0)
            dA[0:hs, :] = da
            dA[hs : hs + 16, :] = jnp.where(
                row == 0, -high, jnp.where(row == 1, high - delta, 0.0)
            ).astype(BF16)
            p = prob[m, e]
            ds = (p.astype(F32) * mm(vA[m], dA[...])).astype(BF16)
            dq = mm(kT[m, 0:hs, :], ds) * scale
            dT[m, pl.ds(pl.multiple_of(e * hs, hs), hs), :] = dq.astype(BF16)
            dkv[0:hs, :] += mm(qT[m, e], ds, NT)
            dkv[hs : 2 * hs, :] += mm(da, p, NT)
            return carry

        lax.fori_loop(0, experts, one, 0)
        g = gate[m, 0:experts, :]
        dg = gate[m, experts : 2 * experts, :]
        dl = g * (dg - jnp.sum(g * dg, 0, keepdims=True))
        dT[m, QR : QR + 16, :] = jnp.concatenate(
            [dl, jnp.zeros((16 - experts, R), F32)], 0
        ).astype(BF16)
        return ga

    def feed(m, out):
        c0 = math.sqrt(2.0 / math.pi)

        def body(i, carry):
            cols = pl.ds(pl.multiple_of(i * FC, FC), FC)
            u = mm(fa[pl.ds(m * R, R), :], up_ref[:, cols])
            u2 = u * u
            t = jnp.tanh(c0 * u * (1.0 + 0.044715 * u2))
            half_up = 0.5 * (1.0 + t)
            a = (u * half_up).astype(BF16)
            act[pl.ds(m * R, R), cols] = a
            gp[pl.ds(m * R, R), cols] = (
                half_up + 0.5 * u * (1.0 - t * t) * (c0 * (1.0 + 3 * 0.044715 * u2))
            ).astype(BF16)
            part = mm(a, down_ref[:, cols], NT)

            @pl.when(i == 0)
            def _():
                out[...] = part

            @pl.when(i > 0)
            def _():
                out[...] += part

            return carry

        lax.fori_loop(0, FF // FC, body, 0)

    def feed_back(m, dout, out):
        def body(i, carry):
            cols = pl.ds(pl.multiple_of(i * FC, FC), FC)
            d = mm(dout[...], down_ref[:, cols])
            d = (d * gp[pl.ds(m * R, R), cols].astype(F32)).astype(BF16)
            gp[pl.ds(m * R, R), cols] = d
            part = mm(d, up_ref[:, cols], NT)

            @pl.when(i == 0)
            def _():
                out[...] = part

            @pl.when(i > 0)
            def _():
                out[...] += part

            return carry

        lax.fori_loop(0, FF // FC, body, 0)

    def norm_back_into(x, k, dz, add, outs):
        g = gain(k)

        def body(s):
            dx, dg = norm_back(x[s, :].astype(F32), g, dz[s, :])
            gacc[k : k + 1, :] += dg
            total = dx if add is None else add[s, :].astype(F32) + dx
            for out in outs:
                out[s, :] = total.astype(out.dtype)

        chunks(R, LC, body)

    norm_to(src_ref, a1, 0, 0)
    norm_to(tgt_ref, a1, R, 0)
    for m in (ENC, DEC):
        kvs[m] = mm(wa_ref[rows.kv, :], a1[m * R : (m + 1) * R, :], NT).astype(BF16)
        exchange(m).start()
    for m in (ENC, DEC):
        z = mm(wa_ref[rows.self_in, :], a1[m * R : (m + 1) * R, :], NT)
        qT[m] = (z[0:QR].astype(BF16).astype(F32) * scale).astype(BF16).reshape(experts, hs, R)
        gates(m, z[QR + 2 * hs :])
    for m in (ENC, DEC):
        kvT[m, :, 0:R] = kvs[m]
        exchange(m).wait()
        kvT[m, :, R:T] = kvr[m]
        set_keys(m, m)

    attend(ENC, False)
    mid[ENC] = src_ref[...].astype(F32) + mm(hT[ENC], wa_ref[rows.o, :], TN)
    norm_to(mid.at[ENC], fa, 0, 1)
    feed(0, top.at[ENC])
    top[ENC] += mid[ENC]
    norm_to(top.at[ENC], mem_ref, 0, 2)
    kvs[CROSS] = mm(wa_ref[rows.ckv, :], mem_ref[...], NT).astype(BF16)
    exchange(CROSS).start()

    attend(DEC, True)
    mid[DEC] = tgt_ref[...].astype(F32) + mm(hT[DEC], wa_ref[rows.o, :], TN)
    norm_to(mid.at[DEC], b2, 0, 3)
    z = mm(wa_ref[rows.cross_in, :], b2[...], NT)
    qT[CROSS] = (z[0:QR].astype(BF16).astype(F32) * scale).astype(BF16).reshape(experts, hs, R)
    gates(CROSS, z[QR:])
    kvT[CROSS, :, 0:R] = kvs[CROSS]
    exchange(CROSS).wait()
    kvT[CROSS, :, R:T] = kvr[CROSS]
    set_keys(CROSS, 0)
    attend(CROSS, False)
    top[DEC] = mid[DEC] + mm(hT[CROSS], wa_ref[rows.co, :], TN)
    norm_to(top.at[DEC], fa, R, 1)
    feed(1, work)
    y_ref[...] = (top[DEC] + work[...]).astype(BF16)

    feed_back(1, ct_ref, work)
    norm_back_into(top.at[DEC], 1, work, ct_ref, (top.at[DEC], workb.at[1]))
    ga_ref[rows.co, :] = attend_back(CROSS, workb[1], rows.co).astype(BF16)
    kvs[3] = dkv[:, R:T].astype(BF16)
    exchange(3).start()
    ga_ref[rows.cross_in, :] = mm(dT[CROSS, 0 : QR + 16, :], b2[...]).astype(BF16)
    work[...] = mm(dT[CROSS, 0 : QR + 16, :], wa_ref[rows.cross_in, :], TN)
    norm_back_into(mid.at[DEC], 3, work, top.at[DEC], (top.at[DEC], workb.at[1]))
    exchange(3).wait()
    dkvc = (dkv[:, 0:R] + kvr[3].astype(F32)).astype(BF16)
    ga_ref[rows.ckv, :] = mm(dkvc, mem_ref[...]).astype(BF16)
    work[...] = mm(dkvc, wa_ref[rows.ckv, :], TN).astype(BF16).astype(F32)
    norm_back_into(top.at[ENC], 2, work, None, (top.at[ENC], workb.at[0]))
    feed_back(0, workb.at[0], work)

    def weights(i, carry):
        cols = pl.ds(pl.multiple_of(i * FC, FC), FC)
        gup_ref[:, cols] = mm(fa[...], gp[:, cols], TN).astype(BF16)
        gdown_ref[:, cols] = (
            mm(workb[0], act[0:R, cols], TN) + mm(ct_ref[...], act[R:T, cols], TN)
        ).astype(BF16)
        return carry

    lax.fori_loop(0, FF // FC, weights, 0)
    norm_back_into(mid.at[ENC], 1, work, top.at[ENC], (top.at[ENC], workb.at[0]))

    go = attend_back(DEC, workb[1], rows.o)
    kvs[5] = dkv[:, R:T].astype(BF16)
    exchange(5).start()
    work[0 : 2 * hs, :] = dkv[:, 0:R]
    dT[DEC, QR + 16 : QR + 16 + 2 * hs, :] = work[0 : 2 * hs, :].astype(BF16)
    kept = dkv[:, 0:R]
    go += attend_back(ENC, workb[0], rows.o)
    ga_ref[rows.o, :] = go.astype(BF16)
    kvs[4] = dkv[:, R:T].astype(BF16)
    exchange(4).start()
    own = (dkv[:, 0:R], kept)
    for m, slot in ((DEC, 5), (ENC, 4)):
        exchange(slot).wait()
        dT[m, QR + 16 : QR + 16 + 2 * hs, :] = (own[m] + kvr[slot].astype(F32)).astype(BF16)
    for part, at in ((rows.q, 0), (rows.r, QR), (rows.kv, QR + 16)):
        n = part.stop - part.start
        ga_ref[part, :] = (
            mm(dT[ENC, at : at + n, :], a1[0:R, :]) + mm(dT[DEC, at : at + n, :], a1[R:T, :])
        ).astype(BF16)
    for m, x, out in ((DEC, tgt_ref, dtgt_ref), (ENC, src_ref, dsrc_ref)):
        work[...] = sum(
            mm(dT[m, at : at + part.stop - part.start, :], wa_ref[part, :], TN)
            for part, at in ((rows.q, 0), (rows.r, QR), (rows.kv, QR + 16))
        )
        norm_back_into(x, 0, work, top.at[m], (out,))
    ga_ref[rows.gain, :] = gacc[...].astype(BF16)


def run_layers(rows, experts, hs, src, tgt, mask, lens, ct, wa, up, down):
    R, W = src.shape
    T, FF, QR = 2 * R, up.shape[1], experts * hs
    vm = pltpu.VMEM
    return pl.pallas_call(
        functools.partial(layer_kernel, rows, experts, hs),
        out_shape=(
            jax.ShapeDtypeStruct((R, W), BF16),
            jax.ShapeDtypeStruct((R, W), BF16),
            jax.ShapeDtypeStruct((R, W), F32),
            jax.ShapeDtypeStruct((R, W), F32),
            jax.ShapeDtypeStruct((rows.total, W), BF16),
            jax.ShapeDtypeStruct((W, FF), BF16),
            jax.ShapeDtypeStruct((W, FF), BF16),
        ),
        in_specs=[pl.BlockSpec(memory_space=vm)] * 8,
        out_specs=[pl.BlockSpec(memory_space=vm)] * 7,
        scratch_shapes=[
            vm((T, W), BF16),
            vm((3, experts, hs, R), BF16),
            vm((3, 2 * hs, T), BF16),
            vm((3, 128, T), BF16),
            vm((3, 128, T), BF16),
            vm((3, T, 128), BF16),
            vm((3, T, 128), BF16),
            vm((128, R), BF16),
            vm((128, R), BF16),
            vm((3, 2 * experts, R), F32),
            vm((3, experts, T, R), BF16),
            vm((3, experts, hs, R), F32),
            vm((3, 8, R), F32),
            vm((3, QR, R), BF16),
            vm((3, QR + 16 + 2 * hs, R), BF16),
            vm((2 * hs, T), F32),
            vm((2, R, W), F32),
            vm((2, R, W), F32),
            vm((T, W), BF16),
            vm((R, W), BF16),
            vm((T, FF), BF16),
            vm((T, FF), BF16),
            vm((R, W), F32),
            vm((2, R, W), BF16),
            vm((16, W), F32),
            vm((6, 2 * hs, R), BF16),
            vm((6, 2 * hs, R), BF16),
            pltpu.SemaphoreType.DMA((6,)),
            pltpu.SemaphoreType.DMA((6,)),
        ],
        compiler_params=pltpu.CompilerParams(
            collective_id=0, has_side_effects=True, vmem_limit_bytes=60 * 2**20
        ),
    )(src, tgt, mask, lens, ct, wa, up, down)


def on_device(
    tokens, self_routes, cross_routes, lengths, cotangent,
    norm_attn, norm_ffn, norm_final, norm_cross,
    router, query_weight, key_weight, value_weight, output_weight, up_weight, down_weight,
    cross_router, cross_query, cross_key, cross_value, cross_output,
):
    section = lax.axis_index("section")
    half = lax.axis_index("head")
    dp = lax.axis_size("dp")
    heads = lax.axis_size("head")
    local, W = tokens.shape[2:]
    el, _, hs = query_weight.shape
    experts = el * heads
    D = query_weight.shape[1]
    rows = Rows(experts * hs, hs)
    swap = [(0, 1), (1, 0)]

    def named(routes):
        ids = jnp.arange(experts, dtype=jnp.int32)[:, None]
        m = ((routes[:, 0][None] == ids) | (routes[:, 1][None] == ids)).astype(F32)
        return jnp.concatenate([m, jnp.zeros((8 - experts, m.shape[1]), F32)], 0)

    def mine(a, axis=0):
        return lax.dynamic_slice_in_dim(a, half * local, local, axis)

    def pick(a, k):
        return lax.dynamic_index_in_dim(a, k, 0, keepdims=False)

    own, other = pick(tokens[0], section), pick(tokens[0], 1 - section)
    routes = mine(self_routes[0], 1)
    own_named, other_named = named(pick(routes, section)), named(pick(routes, 1 - section))
    other = lax.ppermute(other, "section", swap)
    other_named = lax.ppermute(other_named.astype(BF16), "section", swap).astype(F32)
    first = section == 0
    src, tgt = jnp.where(first, own, other), jnp.where(first, other, own)
    mask = jnp.concatenate(
        [
            jnp.where(first, own_named, other_named),
            jnp.where(first, other_named, own_named),
            named(mine(pick(cross_routes, section))),
        ],
        0,
    )
    lens = jnp.broadcast_to(
        jnp.pad(lengths[:, section, 0].astype(F32), (0, 6))[:, None], (8, 128)
    )
    ct = pick(cotangent, section)

    def flat(w):
        return jnp.swapaxes(w, 1, 2).reshape(el * hs, D)

    def pad16(w):
        return jnp.pad(w, ((0, 16 - w.shape[0]), (0, 0)))

    split = jnp.concatenate(
        [
            flat(query_weight), output_weight.reshape(el * hs, D),
            flat(cross_query), cross_output.reshape(el * hs, D),
        ], 0,
    )
    whole = jnp.concatenate(
        [
            key_weight.T, value_weight.T, pad16(router.T),
            cross_key.T, cross_value.T, pad16(cross_router.T),
            pad16(jnp.stack([norm_attn, norm_ffn, norm_final, norm_cross])),
        ], 0,
    )
    n = el * hs
    split = lax.all_gather(lax.all_gather(split, "dp", axis=1, tiled=True), "head", axis=0)
    whole = lax.all_gather(whole, "dp", axis=1, tiled=True)
    q, o, cq, co = (split[:, k * n : (k + 1) * n].reshape(heads * n, W) for k in range(4))
    k2 = 2 * hs
    wa = jnp.concatenate(
        [
            q, whole[: k2 + 16], o, cq,
            whole[2 * k2 + 16 : 2 * k2 + 32], whole[k2 + 16 : 2 * k2 + 16], co,
            whole[2 * k2 + 32 :],
        ], 0,
    )
    ffn = jnp.stack([up_weight, down_weight.T])
    ffn = lax.all_gather(
        lax.all_gather(ffn, "dp", axis=1, tiled=True), "head", axis=2, tiled=True
    )

    memory, y, dsrc, dtgt, ga, gup, gdown = run_layers(
        rows, experts, hs, src, tgt, mask, lens, ct, wa, ffn[0], ffn[1]
    )

    def placed(s, t):
        keep, send = jnp.where(first, s, t), jnp.where(first, t, s).astype(BF16)
        came = lax.ppermute(send, "section", swap).astype(keep.dtype)
        return jnp.where(first, jnp.stack([keep, came]), jnp.stack([came, keep]))

    outputs = placed(memory, y)
    input_grads = placed(dsrc, dtgt)

    def scattered(a, axis):
        return lax.psum_scatter(a, "dp", scatter_dimension=axis, tiled=True)

    gffn = lax.psum_scatter(
        jnp.stack([gup, gdown]), "head", scatter_dimension=2, tiled=True
    )
    gffn = lax.psum(scattered(gffn, 1), "section").astype(F32)
    gs = jnp.concatenate([ga[r].reshape(heads, n, W) for r in (rows.q, rows.o, rows.cq, rows.co)], 1)
    gs = lax.psum_scatter(gs, "head", scatter_dimension=0, tiled=True)[0]
    gw = lax.psum(
        jnp.concatenate([ga[r] for r in (rows.kv, rows.r, rows.ckv, rows.cr, rows.gain)], 0), "head"
    )
    small = lax.psum(scattered(jnp.concatenate([gs, gw], 0), 1), "section").astype(F32)
    gq, go, gcq, gco = (small[k * n : (k + 1) * n].reshape(el, hs, D) for k in range(4))
    rest = small[4 * n :]
    gains = rest[2 * k2 + 32 :]
    return (
        outputs[None], input_grads[None],
        gains[0], gains[1], gains[2], gains[3],
        rest[k2 : k2 + experts].T, jnp.swapaxes(gq, 1, 2), rest[0:hs].T, rest[hs:k2].T, go,
        gffn[0], gffn[1].T,
        rest[2 * k2 + 16 : 2 * k2 + 16 + experts].T, jnp.swapaxes(gcq, 1, 2),
        rest[k2 + 16 : k2 + 16 + hs].T, rest[k2 + 16 + hs : 2 * k2 + 16].T, gco,
    )


def solution(mesh):
    rows = P("section", None, ("dp", "head"), None)
    vector, tall = P("dp"), P("dp", None)
    query, out = P("head", "dp", None), P("head", None, "dp")
    weights = (
        vector, vector, vector, vector,
        tall, query, tall, tall, out, P("dp", "head"), P("head", "dp"),
        tall, query, tall, tall, out,
    )
    return jax.shard_map(
        on_device,
        mesh=mesh,
        in_specs=(
            rows, P("section", None, "dp", None), P(None, "dp", None), P(None, None, "dp"),
            P(None, ("dp", "head"), None), *weights,
        ),
        out_specs=(rows, rows, *weights),
        check_vma=False,
    )
```

time: 1540 us -> 443 us (0.29)
  matrix products: 352 us -> 0 us
  waiting for transfers between devices: 509 us -> 240 us
  other arithmetic: 254 us -> 26 us
  blocking collectives: 186 us -> 33.5 us
  local copies, waits for them, and re-layouts: 133 us -> 32.9 us
  Pallas kernels: 0 us -> 90.4 us
  starting transfers between devices: 70.4 us -> 4.56 us
    dot_general x131 -> x0, matrix products: 338 us -> none  [the longest x12 38.2 us: single(): jnp.einsum('eqh,kh->eqk', query_one, key_one, preferred_element_type=jnp....]
    all_gather x20 -> x3, waiting for transfers between devices: 188 us -> 62 us  [the longest x1 49.9 us: on_device(): lax.all_gather(lax.all_gather(ffn, 'dp', axis=1, tiled=True), 'head', axi...]
    all_gather x13 -> x2, blocking collectives: 152 us -> 33.5 us  [the longest x1 19.1 us: on_device(): lax.all_gather(split, 'dp', axis=1, tiled=True)]
    reduce_sum x101 -> x0, other arithmetic: 100 us -> none  [the longest x14 18.9 us: layer_norm(): jnp.mean(centred * centred, -1, keepdims=True) + EPSILON]
    pallas_call x0 -> x1, Pallas kernels: none -> 90.4 us  [run_layers(): pl.pallas_call(functools.partial(layer_kernel, rows, experts, hs), out_sh...]
    unnamed x613 -> x55, local copies, waits for them, and re-layouts: 77.1 us -> 4.74 us
    all_to_all x13 -> x0, starting transfers between devices: 55.8 us -> none  [summed_on_arrival(): lax.all_to_all(blocks, axis, split_axis=0, concat_axis=0, tiled=True)]
    psum x6 -> x2, waiting for transfers between devices: 85.7 us -> 36.1 us  [the longest x1 23.8 us: on_device(): lax.psum(scattered(jnp.concatenate([gs, gw], 0), 1), 'section').astype(F32)]
  transfers between devices with their start and end apart: 61 -> 13, of which waited for: 41 -> 9; matrix products, arithmetic and copies ran while one was open for 31% -> 9% of each run, Pallas kernels for 0% -> 0%
where the time goes in v1:
time: 443 us; the launch traced here: 442 us
  waiting for transfers between devices  240 us (54%)
  Pallas kernels  90.4 us (20%)
  blocking collectives  33.5 us (8%)
  local copies, waits for them, and re-layouts  32.9 us (7%)
  other arithmetic  26 us (6%)
  between operations  14.3 us (3%)
  starting transfers between devices  4.56 us (1%)
    pallas_call x1, Pallas kernels, run_layers(): pl.pallas_call(functools.partial(layer_kernel, rows, experts, hs), out_sh...  90.4 us
    reduce_scatter x1, waiting for transfers between devices, on_device(): lax.psum_scatter(jnp.stack([gup, gdown]), 'head', scatter_dimension=2, ti...  54.4 us
    reduce_scatter x2, waiting for transfers between devices, scattered(): return lax.psum_scatter(a, 'dp', scatter_dimension=axis, tiled=True)  53.8 us
    all_gather x1, waiting for transfers between devices, on_device(): lax.all_gather(lax.all_gather(ffn, 'dp', axis=1, tiled=True), 'head', axi...  49.9 us
    psum x1, waiting for transfers between devices, on_device(): lax.psum(scattered(jnp.concatenate([gs, gw], 0), 1), 'section').astype(F32)  23.8 us
    reduce_scatter x1, waiting for transfers between devices, on_device(): gs = lax.psum_scatter(gs, 'head', scatter_dimension=0, tiled=True)[0]  21.9 us
    all_gather x1, blocking collectives, on_device(): lax.all_gather(split, 'dp', axis=1, tiled=True)  19.1 us
    all_gather x1, blocking collectives, on_device(): whole = lax.all_gather(whole, 'dp', axis=1, tiled=True)  14.4 us
  transfers between devices with their start and end apart: 13, of which 9 were waited for; matrix products, arithmetic and copies ran while one was open for 9% of the time, Pallas kernels for 0%

profile of v1, /device:TPU:0, one launch (start us, length us, event | category | flops | bytes accessed | tf_op | source)
XLA Modules:
  0.0 441.7 jit_solution(7561225310623506019)
XLA Ops:
  7.3 1.8 pad_maximum_fusion.4
  12.8 19.1 %all_gather.18 = bf16[512,512]{0,1:T(8,128)(2,1)} all-gather(bf16[512,64]{0,1:T(8,128)(2,1)S(1)} %pad_maximum_fusion.5), channel_id=1, replica_groups=mesh['section'=2,'dp'=8,'head'=2] {'dp'}, dimensions={1}, use_global_device_ids=true | all-gather | bytes 589824 | tf_op jit(solution)/shard_map/all_gather | solution.py:467
  31.9 12.1 %all-gather.5.cloned.1.call-done = bf16[2,512,1024]{2,1,0:T(8,128)(2,1)} async-done(((bf16[2,64,1024]{2,1,0:T(8,128)(2,1)}), bf16[2,512,1024]{2,1,0:T(8,128)(2,1)}) %all-gather.5.cloned.1.call-update) | async-done | bytes 2097168 | tf_op jit(solution)/shard_map/all_gather | solution.py:480
  44.9 1.5 collective-permute-start.1
  48.4 14.4 %all_gather.21 = bf16[304,512]{0,1:T(8,128)(2,1)S(1)} all-gather(bf16[304,64]{0,1:T(8,128)(2,1)S(1)} %concatenate.66), channel_id=1, replica_groups=mesh['section'=2,'dp'=8,'head'=2] {'dp'}, dimensions={1}, use_global_device_ids=true | all-gather | bytes 350208 | tf_op jit(solution)/shard_map/all_gather | solution.py:468
  66.0 1.0 copy.109
  67.0 1.0 copy.107
  69.7 1.4 maximum_maximum_fusion.mask_ref
  71.0 2.1 bitcast_select_fusion
  73.2 1.6 copy.104
  75.0 49.9 %all-gather.7.cloned.1.call-done = bf16[2,512,2048]{2,1,0:T(8,128)(2,1)} async-done(((bf16[2,512,1024]{2,1,0:T(8,128)(2,1)}), bf16[2,512,2048]{2,1,0:T(8,128)(2,1)}) %all-gather.7.cloned.1.call-update) | async-done | bytes 4194320 | tf_op jit(solution)/shard_map/all_gather | solution.py:479
  124.9 4.8 %slice_bitcast_fusion = (bf16[512,2048]{1,0:T(8,128)(2,1)}, bf16[512,2048]{1,0:T(8,128)(2,1)}) fusion(bf16[2,512,2048]{2,1,0:T(8,128)(2,1)} %all-gather.7.cloned.1.call-done), kind=kLoop, calls=%fused_computation.1 | loop fusion | bytes 8388608 | tf_op jit(solution)/shard_map/squeeze | solution.py:484
  130.4 90.4 %shard_map.340 = (bf16[512,512]{1,0:T(8,128)(2,1)}, bf16[512,512]{1,0:T(8,128)(2,1)}, f32[512,512]{1,0:T(8,128)}, f32[512,512]{1,0:T(8,128)}, bf16[1328,512]{1,0...) custom-call(bf16[512,512]{1,0:T(8,128)(2,1)} %get-tuple-element.95.src_ref, ...), custom_call_target="tpu_custom_call" | custom-call | tf_op jit(solution)/shard_map/pallas_call | solution.py:349
  226.9 2.0 copy.93
  229.7 2.3 pad_maximum_fusion.1
  232.1 4.0 pad_maximum_fusion
  236.1 12.3 %all-reduce.10.cloned.1.call-done = bf16[304,512]{1,0:T(8,128)(2,1)} async-done(((bf16[304,512]{1,0:T(8,128)(2,1)}), bf16[304,512]{1,0:T(8,128)(2,1)}) %all-reduce.10.cloned.1.call-update) | async-done | bytes 311312 | tf_op jit(solution)/shard_map/psum | solution.py:504
  248.4 1.2 copy.95
  249.6 21.9 %reduce-scatter.5.cloned.1.call-done = bf16[1,512,512]{1,2,0:T(8,128)(2,1)} async-done(((bf16[2,512,512]{1,2,0:T(8,128)(2,1)}), bf16[1,512,512]{1,2,0:T(8,128)(2,1)}) %reduce-scatter.5.cloned.1.call-update) | async-done | bytes 524304 | tf_op jit(solution)/shard_map/reduce_scatter | solution.py:503
  271.5 2.0 pad_maximum_fusion.2
  273.6 54.4 %reduce-scatter.9.cloned.1.call-done = bf16[2,512,1024]{2,1,0:T(8,128)(2,1)} async-done(((bf16[2,512,2048]{2,1,0:T(8,128)(2,1)}), bf16[2,512,1024]{2,1,0:T(8,128)(2,1)}) %reduce-scatter.9.cloned.1.call-update) | async-done | bytes 2097168 | tf_op jit(solution)/shard_map/reduce_scatter | solution.py:498
  328.1 1.4 select_bitcast_fusion.1
  329.5 1.5 collective-permute-start.2
  331.0 0.9 select_convert_fusion
  332.7 11.6 %collective-permute-done.2 = bf16[512,512]{1,0:T(8,128)(2,1)S(1)} collective-permute-done((bf16[512,512]{1,0:T(8,128)(2,1)S(1)}, bf16[512,512]{1,0:T(8,128)(2,1)S(1)}, u32[]{:S(2)}, u32[]{:S(2)}) %collective-permute-start.2) | collective-permute-done | bytes 524320 | tf_op jit(solution)/shard_map/ppermute | solution.py:489
  344.4 1.1 maximum_select_fusion.1
  345.5 17.2 %reduce-scatter.7.cloned.1.call-done = bf16[816,64]{0,1:T(8,128)(2,1)} async-done(((bf16[816,512]{0,1:T(8,128)(2,1)}), bf16[816,64]{0,1:T(8,128)(2,1)}) %reduce-scatter.7.cloned.1.call-update) | async-done | bytes 104464 | tf_op jit(solution)/shard_map/reduce_scatter | solution.py:496
  362.7 36.6 %reduce-scatter.11.cloned.1.call-done = bf16[2,64,1024]{2,1,0:T(8,128)(2,1)} async-done(((bf16[2,512,1024]{2,1,0:T(8,128)(2,1)}), bf16[2,64,1024]{2,1,0:T(8,128)(2,1)}) %reduce-scatter.11.cloned.1.call-update) | async-done | bytes 262160 | tf_op jit(solution)/shard_map/reduce_scatter | solution.py:496
  399.3 1.2 bitcast_convert_fusion
  400.5 1.6 maximum_select_fusion
  402.1 23.8 %all-reduce.12.cloned.1.call-done = (bf16[816,64]{0,1:T(8,128)(2,1)}, bf16[2,64,1024]{2,1,0:T(8,128)(2,1)}) async-done(((bf16[816,64]{0,1:T(8,128)(2,1)}, bf16[2,64,1024]{2,1,0:T(8,128)(2,1)}), (bf16[816,64]{0,1:T(8,128)(2,1)}, bf16[2,64,1024]{2,1,0:T(8,128)(2,1)})) %all-reduce.12.cloned.1.call-update) | async-done | bytes 366608 | tf_op jit(solution)/shard_map/psum | solution.py:507
  433.4 1.0 convert_element_type.40
  (130 shorter events, 28.4 us)
Async XLA Ops:
  7.2 57.6 %copy-start = (bf16[2,512,512]{2,1,0:T(8,128)(2,1)S(1)}, bf16[2,512,512]{2,1,0:T(8,128)(2,1)}, u32[]{:S(2)}) copy-start(bf16[2,512,512]{2,1,0:T(8,128)(2,1)} %param.25) | copy-start | bytes 3145732
  7.2 36.9 %all-gather.5.cloned.1.call-start = ((), (), s32[]{:S(2)}) async-start(), calls=%async_computation.4 | async-start | bytes 2359296 | tf_op jit(solution)/shard_map/all_gather | solution.py:480
  9.0 35.1 %copy-start.12 = (s32[1,2,1024,2]{2,3,1,0:T(2,128)S(1)}, s32[1,2,1024,2]{2,3,1,0:T(2,128)}, u32[]{:S(2)}) copy-start(s32[1,2,1024,2]{2,3,1,0:T(2,128)} %param.22) | copy-start | bytes 49156
  9.0 37.3 %copy-start.7 = (bf16[1,2,512,512]{3,2,1,0:T(8,128)(2,1)S(1)}, bf16[1,2,512,512]{3,2,1,0:T(8,128)(2,1)}, u32[]{:S(2)}) copy-start(bf16[1,2,512,512]{3,2,1,0:T(8,128)(2,1)} %param.21) | copy-start | bytes 3145732
  9.1 64.1 %all-gather.9.cloned.1.call-start = ((), (), s32[]{:S(2)}) async-start(), calls=%async_computation.11 | async-start | bytes 1572864 | tf_op jit(solution)/shard_map/all_gather | solution.py:467
  12.7 34.3 %copy-start.15 = (bf16[64]{0:T(256)(128)(2,1)S(1)}, bf16[64]{0:T(256)(128)(2,1)}, u32[]{:S(2)}) copy-start(bf16[64]{0:T(256)(128)(2,1)} %param.29) | copy-start | bytes 388
  12.7 34.3 %copy-start.16 = (bf16[64]{0:T(256)(128)(2,1)S(1)}, bf16[64]{0:T(256)(128)(2,1)}, u32[]{:S(2)}) copy-start(bf16[64]{0:T(256)(128)(2,1)} %param.28) | copy-start | bytes 388
  12.7 34.3 %copy-start.17 = (bf16[64]{0:T(256)(128)(2,1)S(1)}, bf16[64]{0:T(256)(128)(2,1)}, u32[]{:S(2)}) copy-start(bf16[64]{0:T(256)(128)(2,1)} %param.27) | copy-start | bytes 388
  12.7 34.3 %copy-start.18 = (bf16[64]{0:T(256)(128)(2,1)S(1)}, bf16[64]{0:T(256)(128)(2,1)}, u32[]{:S(2)}) copy-start(bf16[64]{0:T(256)(128)(2,1)} %param.26) | copy-start | bytes 388
  12.7 34.4 %copy-start.13 = (bf16[64,4]{0,1:T(4,128)(2,1)S(1)}, bf16[64,4]{0,1:T(4,128)(2,1)}, u32[]{:S(2)}) copy-start(bf16[64,4]{0,1:T(4,128)(2,1)} %param.30) | copy-start | bytes 1540
  12.7 34.6 %copy-start.14 = (bf16[64,4]{0,1:T(4,128)(2,1)S(1)}, bf16[64,4]{0,1:T(4,128)(2,1)}, u32[]{:S(2)}) copy-start(bf16[64,4]{0,1:T(4,128)(2,1)} %param.37) | copy-start | bytes 1540
  31.8 15.6 %copy-start.8 = (bf16[64,64]{1,0:T(8,128)(2,1)S(1)}, bf16[64,64]{1,0:T(8,128)(2,1)}, u32[]{:S(2)}) copy-start(bf16[64,64]{1,0:T(8,128)(2,1)} %param.32) | copy-start | bytes 24580
  31.8 15.6 %copy-start.9 = (bf16[64,64]{1,0:T(8,128)(2,1)S(1)}, bf16[64,64]{1,0:T(8,128)(2,1)}, u32[]{:S(2)}) copy-start(bf16[64,64]{1,0:T(8,128)(2,1)} %param.33) | copy-start | bytes 24580
  31.8 15.6 %copy-start.10 = (bf16[64,64]{1,0:T(8,128)(2,1)S(1)}, bf16[64,64]{1,0:T(8,128)(2,1)}, u32[]{:S(2)}) copy-start(bf16[64,64]{1,0:T(8,128)(2,1)} %param.39) | copy-start | bytes 24580
  31.8 15.6 %copy-start.11 = (bf16[64,64]{1,0:T(8,128)(2,1)S(1)}, bf16[64,64]{1,0:T(8,128)(2,1)}, u32[]{:S(2)}) copy-start(bf16[64,64]{1,0:T(8,128)(2,1)} %param.40) | copy-start | bytes 24580
  31.9 93.1 %all-gather.7.cloned.1.call-start = ((), (), s32[]{:S(2)}) async-start(), calls=%async_computation.5 | async-start | bytes 6291456 | tf_op jit(solution)/shard_map/all_gather | solution.py:479
  44.1 204.3 %all-reduce.10.cloned.1.call-start = ((), (), s32[]{:S(2)}) async-start(), calls=%async_computation.7 | async-start | bytes 622592 | tf_op jit(solution)/shard_map/psum | solution.py:504
  44.9 24.1 %collective-permute-start.1 = (bf16[8,512]{1,0:T(8,128)(2,1)}, bf16[8,512]{1,0:T(8,128)(2,1)}, u32[]{:S(2)}, u32[]{:S(2)}) collective-permute-start(bf16[8,512]{1,0:T(8,128)(2,1)} %convert_convert_fusion), channel_id=1, source_target_pairs={{0,16},{16,0},{1,17},{17,1},{2,18},{18,2},{3,19},{19,3},{4,20},{20... | collective-permute-start | bytes 24584 | tf_op jit(solution)/shard_map/ppermute | solution.py:431
  46.4 24.7 %collective-permute-start = (bf16[512,512]{1,0:T(8,128)(2,1)S(1)}, bf16[512,512]{1,0:T(8,128)(2,1)}, u32[]{:S(2)}, u32[]{:S(2)}) collective-permute-start(bf16[512,512]{1,0:T(8,128)(2,1)S(1)} %dynamic-slice_bitcast_fusion.1), channel_id=1, source_target_pairs={{0,16},{16,0},{1,17},{17,1},{2,18},{18,2},{3,19},{19,3},{4,20},{20... | collective-permute-start | bytes 1572872 | tf_op jit(solution)/shard_map/ppermute | solution.py:430
  75.0 54.7 %copy-start.5 = (bf16[1328,512]{1,0:T(8,128)(2,1)}, bf16[1328,512]{1,0:T(8,128)(2,1)S(1)}, u32[]{:S(2)}) copy-start(bf16[1328,512]{1,0:T(8,128)(2,1)S(1)} %constant_dynamic-update-slice_fusion.wa_ref) | copy-start | bytes 4079620
  220.8 3.5 copy-start.6
  224.3 47.2 %reduce-scatter.5.cloned.1.call-start = ((), (), s32[]{:S(2)}) async-start(), calls=%async_computation.6 | async-start | bytes 1572864 | tf_op jit(solution)/shard_map/reduce_scatter | solution.py:503
  226.9 5.2 %copy-start.4 = (bf16[512,2048]{1,0:T(8,128)(2,1)S(1)}, bf16[512,2048]{1,0:T(8,128)(2,1)}, u32[]{:S(2)}) copy-start(bf16[512,2048]{1,0:T(8,128)(2,1)} %get-tuple-element.30) | copy-start | bytes 6291460
  232.0 96.0 %reduce-scatter.9.cloned.1.call-start = ((), (), s32[]{:S(2)}) async-start(), calls=%async_computation.9 | async-start | bytes 6291456 | tf_op jit(solution)/shard_map/reduce_scatter | solution.py:498
  236.1 126.7 %reduce-scatter.7.cloned.1.call-start = ((), (), s32[]{:S(2)}) async-start(), calls=%async_computation.8 | async-start | bytes 1032192 | tf_op jit(solution)/shard_map/reduce_scatter | solution.py:496
  273.6 125.7 %reduce-scatter.11.cloned.1.call-start = ((), (), s32[]{:S(2)}) async-start(), calls=%async_computation.10 | async-start | bytes 2359296 | tf_op jit(solution)/shard_map/reduce_scatter | solution.py:496
  328.0 3.0 copy-start.1
  328.0 3.0 copy-start.2
  328.0 97.9 %all-reduce.12.cloned.1.call-start = ((), (), s32[]{:S(2)}) async-start(), calls=%async_computation.12 | async-start | bytes 753664 | tf_op jit(solution)/shard_map/psum | solution.py:507
  328.0 4.5 %copy-start.3 = (f32[512,512]{1,0:T(8,128)S(1)}, f32[512,512]{1,0:T(8,128)}, u32[]{:S(2)}) copy-start(f32[512,512]{1,0:T(8,128)} %get-tuple-element.28) | copy-start | bytes 3145732
  329.5 14.9 %collective-permute-start.2 = (bf16[512,512]{1,0:T(8,128)(2,1)S(1)}, bf16[512,512]{1,0:T(8,128)(2,1)S(1)}, u32[]{:S(2)}, u32[]{:S(2)}) collective-permute-start(bf16[512,512]{1,0:T(8,128)(2,1)S(1)} %get-tuple-element.103), channel_id=1, source_target_pairs={{0,16},{16,0},{1,17},{17,1},{2,18},{18,2},{3,19},{19,3},{4,20},{20... | collective-permute-start | bytes 1572872 | tf_op jit(solution)/shard_map/ppermute | solution.py:489
  332.0 67.4 %collective-permute-start.3 = (bf16[512,512]{1,0:T(8,128)(2,1)}, bf16[512,512]{1,0:T(8,128)(2,1)}, u32[]{:S(2)}, u32[]{:S(2)}) collective-permute-start(bf16[512,512]{1,0:T(8,128)(2,1)} %select_convert_fusion), channel_id=1, source_target_pairs={{0,16},{16,0},{1,17},{17,1},{2,18},{18,2},{3,19},{19,3},{4,20},{20... | collective-permute-start | bytes 1572872 | tf_op jit(solution)/shard_map/ppermute | solution.py:489
Sparse Core Ops, SparseCore 0:
  10.2 33.7 all-gather.4
  45.6 20.9 all-gather.8
  68.2 56.7 all-gather.6
  224.4 23.9 all-reduce.9
  251.1 20.3 reduce-scatter.4
  273.6 54.2 reduce-scatter.8
  330.9 31.7 reduce-scatter.6
  365.0 34.2 reduce-scatter.10
  401.6 24.1 all-reduce.11
